TPU v7x, 128 devices: a whole 4x4x4 slice. The times are simulated.
128 devices in a mesh: region: 4 (over z_hi, core), dev: 32 (over x, y, z_lo).
Axes of the slice: x: 4, y: 4, z: 4 (z_hi: 2, z_lo: 2; z = z_hi * 2 + z_lo), core: 2. Of those that a mesh axis runs over, the one named last changes fastest.
Arguments:
- science: float32 [4, 32, 2, 1024, 2, 128], P('region', 'dev'), may hold values from -6 to 6, as said below
- coadd: float32 [4, 4096, 2, 128], P('region', 'dev'), may hold values from -6 to 6, as said below
- coefficients: float32 [4, 32, 2, 31, 3], P('region', 'dev'), may hold values from -1 to 1
- strip_start: int32 [4, 32, 2], P('region', 'dev'), may hold values from 0 to 24, as said below
Outputs:
- patch_sums: float32 [4, 4096, 2, 128], P('region', 'dev')
Inputs may be any that keep to these rules, and one draw needn't show every extreme that they name: Strip e of a device covers blocks strip_start .. strip_start + 7 of its region; the two strips of one device cover 2 * 8 different blocks; no block is covered by more than 32 strips, and in every region some block is covered by a strip of every device of the region; some region has a strip starting at 0 and some region one starting at 24. `science`: plane 1 holds positive variances. `coadd`: plane 1 holds positive variances.
All inputs are finite; a program needn't handle non-finite values.
Results may differ from a plain program's by a relative error of at most 0.0001.
Values sent between devices are 32-bit elements; how exact they have to be, the bound alone decides.
A program may use at most 64 MiB of HBM per device.

v0:
```python
import jax
import jax.numpy as jnp
from jax import lax
from jax.sharding import PartitionSpec as P

BLK = 128
CW = 128
EXP_DEV = 2
KSIZE = 21
NPROF = 12
SPREADS = (1.0, 2.0, 4.0)
DEGREES = (4, 3, 2)


def padded_2(cells, sides, width):
    for axis, dim in sides:
        count = lax.axis_size(axis)
        ends = count - 1
        head = lax.slice_in_dim(cells, 0, width, axis=dim)
        tail = lax.slice_in_dim(cells, cells.shape[dim] - width, cells.shape[dim], axis=dim)
        cells = jnp.concatenate(
            [
                lax.ppermute(tail, axis, [(i, (i + 1) % count) for i in range(ends)]),
                cells,
                lax.ppermute(head, axis, [((i + 1) % count, i) for i in range(ends)]),
            ],
            axis=dim,
        )
    return cells


def profile_values(offset, spread, exponent):
    half_width = (KSIZE - 1) // 2
    scaled = offset / half_width
    return scaled**exponent * jnp.exp(-offset * offset / (2.0 * spread * spread))


def profile_list():
    entries = []
    for spread, degree in zip(SPREADS, DEGREES):
        for exponent in range(degree + 1):
            entries.append((spread, exponent))
    return entries


def profile_norms():
    taps = jnp.arange(KSIZE, dtype=jnp.float32) - (KSIZE - 1) // 2
    return [
        jnp.sum(jnp.abs(profile_values(taps, spread, exponent)))
        for spread, exponent in profile_list()
    ]


def basis_list():
    listing = []
    offset = 0
    for degree in DEGREES:
        for vertical in range(degree + 1):
            for across in range(degree + 1 - vertical):
                listing.append((offset + vertical, offset + across))
        offset = offset + degree + 1
    return listing


def across_matrix(norm_values):
    half_width = (KSIZE - 1) // 2
    source = jnp.arange(CW, dtype=jnp.float32)[:, None]
    target = jnp.arange(CW, dtype=jnp.float32)[None, :]
    offset = source - target
    inside = jnp.abs(offset) <= half_width
    blocks = []
    for (spread, exponent), norm_value in zip(profile_list(), norm_values):
        blocks.append(jnp.where(inside, profile_values(offset, spread, exponent) / norm_value, 0.0))
    return jnp.concatenate(blocks, axis=1)


def down_matrix(spread, exponent, norm_value, out_rows):
    half_width = (KSIZE - 1) // 2
    output_rows = jnp.arange(out_rows, dtype=jnp.float32)[:, None]
    input_rows = jnp.arange(out_rows + 2 * half_width, dtype=jnp.float32)[None, :]
    offset = input_rows - output_rows - half_width
    inside = jnp.abs(offset) <= half_width
    return jnp.where(inside, profile_values(offset, spread, exponent) / norm_value, 0.0)


def kernel_norm_list(profile_sums):
    return jnp.stack(
        [profile_sums[upright] * profile_sums[across] for upright, across in basis_list()]
    )


def strip_terms(window, strip_data, spatial_terms, wide_matrix, norm_values, profile_sums):
    half_width = (KSIZE - 1) // 2
    out_rows = strip_data.shape[0]
    block_count = out_rows // BLK
    listing = basis_list()
    flux_plane = window[:, 0, :]
    in_rows = flux_plane.shape[0]
    across_all = jnp.dot(flux_plane, wide_matrix, precision=lax.Precision.HIGHEST).reshape(
        in_rows, NPROF, CW
    )
    column_coords = (2.0 * jnp.arange(CW, dtype=jnp.float32) + 1.0) / CW - 1.0
    row_coords = (2.0 * jnp.arange(out_rows, dtype=jnp.float32) + 1.0) / out_rows - 1.0
    row_blocks = row_coords.reshape(block_count, BLK, 1)
    model_blocks = jnp.zeros((block_count, BLK, CW), jnp.float32)
    for vertical, (spread, exponent) in enumerate(profile_list()):
        flat_part = jnp.zeros((in_rows, CW), jnp.float32)
        sloped = jnp.zeros((in_rows, CW), jnp.float32)
        for number, (upright, across) in enumerate(listing):
            if upright == vertical:
                flat_part = (
                    flat_part
                    + (spatial_terms[number, 0] + spatial_terms[number, 1] * column_coords[None, :])
                    * across_all[:, across, :]
                )
                sloped = sloped + spatial_terms[number, 2] * across_all[:, across, :]
        paired = jnp.stack([flat_part, sloped])
        pieces = jnp.stack(
            [
                paired[:, block_index * BLK : block_index * BLK + BLK + 2 * half_width]
                for block_index in range(block_count)
            ],
            axis=1,
        )
        matrix_rows = down_matrix(spread, exponent, norm_values[vertical], BLK)
        smoothed = jnp.einsum("oi,tbic->tboc", matrix_rows, pieces, precision=lax.Precision.HIGHEST)
        model_blocks = model_blocks + smoothed[0] + row_blocks * smoothed[1]
    model_image = model_blocks.reshape(out_rows, CW)
    kernel_norms = kernel_norm_list(profile_sums)
    kernel_sum = (
        jnp.sum(spatial_terms[:, 0] * kernel_norms)
        + jnp.sum(spatial_terms[:, 1] * kernel_norms) * column_coords[None, :]
        + jnp.sum(spatial_terms[:, 2] * kernel_norms) * row_coords[:, None]
    )
    variance = (
        strip_data[:, 1, :]
        + kernel_sum * kernel_sum * window[half_width : half_width + out_rows, 1, :]
    )
    weight = 1.0 / variance
    return jnp.stack([(strip_data[:, 0, :] - model_image) * weight, weight], axis=1)


def per_device(science, coadd, coefficients, strip_start):
    half_width = (KSIZE - 1) // 2
    strip_rows = science.shape[3]
    groups = lax.axis_size("dev")
    norm_values = profile_norms()
    taps = jnp.arange(KSIZE, dtype=jnp.float32) - half_width
    profile_sums = jnp.stack(
        [
            jnp.sum(profile_values(taps, spread, exponent)) / norm_value
            for (spread, exponent), norm_value in zip(profile_list(), norm_values)
        ]
    )
    wide_matrix = across_matrix(norm_values)
    region_band = lax.all_gather(coadd[0], "dev", axis=0, tiled=True)
    edge_rows = jnp.concatenate([region_band[:half_width], region_band[-half_width:]], axis=0)
    extended = padded_2(edge_rows, (("region", 0),), half_width)
    padded = jnp.concatenate([extended[:half_width], region_band, extended[-half_width:]], axis=0)
    dense_sums = jnp.zeros((groups * BLK, 2, CW), jnp.float32)
    for strip_number in range(EXP_DEV):
        first_row = strip_start[0, 0, strip_number] * BLK
        window = lax.dynamic_slice_in_dim(padded, first_row, strip_rows + 2 * half_width, 0)
        contributions = strip_terms(
            window,
            science[0, 0, strip_number],
            coefficients[0, 0, strip_number],
            wide_matrix,
            norm_values,
            profile_sums,
        )
        current = lax.dynamic_slice_in_dim(dense_sums, first_row, strip_rows, 0)
        dense_sums = lax.dynamic_update_slice_in_dim(
            dense_sums, current + contributions, first_row, 0
        )
    result = lax.psum_scatter(dense_sums, "dev", scatter_dimension=0, tiled=True)
    return result[None]


def solution(mesh):
    placed = (
        P("region", "dev", None, None, None, None),
        P("region", "dev", None, None),
        P("region", "dev", None, None, None),
        P("region", "dev", None),
    )
    return jax.shard_map(
        per_device,
        mesh=mesh,
        in_specs=placed,
        out_specs=P("region", "dev", None, None),
        check_vma=False,
    )
```

profile of v0, /device:TPU:0, one launch (start us, length us, event | category | flops | bytes accessed | tf_op | source)
XLA Modules:
  0.0 492.1 jit_solution(11164558315770203030)
XLA Ops:
  6.5 1.7 copy.34
  44.6 1.4 multiply_add_fusion.66
  48.5 1.4 multiply_add_fusion.39
  53.6 1.3 multiply_add_fusion.62
  54.9 1.3 multiply_add_fusion.63
  61.2 1.3 multiply_add_fusion.58
  63.7 1.3 multiply_add_fusion.47
  72.2 1.3 multiply_add_fusion.45
  85.5 1.4 multiply_add_fusion.100
  95.1 1.3 multiply_add_fusion.92
  101.4 1.3 multiply_add_fusion.74
  104.0 1.3 multiply_add_fusion.89
  108.6 1.3 multiply_add_fusion.79
  116.8 1.3 multiply_add_fusion.77
  123.0 1.4 multiply_add_fusion.85
  136.1 33.3 %all-gather.3.cloned.1.call-done = f32[1,4096,2,128]{3,1,2,0:T(8,128)} async-done(((f32[1,128,2,128]{3,1,2,0:T(8,128)}), f32[1,4096,2,128]{3,1,2,0:T(8,128)}) %all-gather.3.cloned.1.call-update) | async-done | bytes 4194320 | tf_op jit(solution)/shard_map/all_gather | solution.py:156
  170.1 1.3 collective-permute-start
  171.4 1.3 collective-permute-start.1
  175.2 4.0 collective-permute-done.1
  179.2 13.4 %concatenate.6 = f32[4116,2,128]{2,0,1:T(8,128)} concatenate(f32[10,2,128]{2,0,1:T(8,128)S(1)} %collective-permute-done, f32[4096,2,128]{2,0,1:T(8,128)} %bitcast.1688, f32[10,2,128]{2,0,1:T(8,128)S(1)} %collective-permute-done.1), dimensions={0} | concatenate | bytes 8429568 | tf_op jit(solution)/shard_map/concatenate | solution.py:159
  192.6 6.2 %fusion.25 = f32[1044,12,128]{2,0,1:T(8,128)S(1)} fusion(f32[12,128,128]{2,1,0:T(8,128)S(1)} %bitcast.1689, f32[4116,2,128]{2,0,1:T(8,128)} %concatenate.6, s32[]{:T(128)S(6)} %select_n.126), kind=kOutput, calls=%fused_computation.402 | convolution fusion | flops 2463105024 | bytes 7737348 | tf_op jit(solution)/shard_map/dot_general | solution.py:99
  198.8 6.5 %fusion.26 = f32[1044,12,128]{2,0,1:T(8,128)S(1)} fusion(f32[12,128,128]{2,1,0:T(8,128)S(1)} %bitcast.1690, f32[4116,2,128]{2,0,1:T(8,128)} %concatenate.6, s32[]{:T(128)S(6)} %select_n.99), kind=kOutput, calls=%fused_computation.416 | convolution fusion | flops 2463105024 | bytes 7737348 | tf_op jit(solution)/shard_map/dot_general | solution.py:99
  205.3 2.2 multiply_add_fusion.17
  207.5 5.6 %multiply_add_fusion.16 = (f32[1,1044,128]{2,1,0:T(8,128)S(1)}, f32[1,1044,128]{2,1,0:T(8,128)S(1)}, f32[1,1044,128]{2,1,0:T(8,128)S(1)}, f32[1,1044,128]{2,1,0:T(8,128)S(1)}) fusion(f32[1044,12,128]{2,0,1:T(8,128)S(1)} %fusion.25, f32[]{:T(128)} %bitcast.317, f32[]{:T(128)} %bitcast.316, f32[]{:T(128)} %bitcast.315, f32[]{:T(128)} %bitcast.314, ...), kind=kLoop, calls=%fused_computation.433 | loop fusion | flops 1870848 | bytes 5345316 | tf_op jit(solution)/shard_map/add | solution.py:116
  213.3 2.1 convolution_bitcast_fusion.11
  215.5 2.2 multiply_add_fusion.15
  217.6 5.8 %multiply_add_fusion.14 = (f32[1,1044,128]{2,1,0:T(8,128)S(1)}, f32[1,1044,128]{2,1,0:T(8,128)S(1)}, f32[1,1044,128]{2,1,0:T(8,128)S(1)}) fusion(f32[1044,12,128]{2,0,1:T(8,128)S(1)} %fusion.25, f32[]{:T(128)} %bitcast.341, f32[]{:T(128)} %bitcast.340, f32[]{:T(128)} %bitcast.339, f32[]{:T(128)} %bitcast.338, f32[]{:T(128)} %bitcast.362, f32[]{:T(128)} %bitcast.361, ...), kind=kLoop, calls=%fused_computation.431 | loop fusion | flops 2004480 | bytes 4810788 | tf_op jit(solution)/shard_map/add | solution.py:116
  223.6 1.7 convolution_bitcast_fusion.10
  225.4 2.1 multiply_add_fusion.13
  227.6 1.8 convolution_bitcast_fusion.9
  229.5 2.7 multiply_add_fusion.11
  232.4 1.8 convolution_bitcast_fusion.8
  234.7 1.8 convolution_bitcast_fusion.7
  236.7 1.8 convolution_bitcast_fusion.6
  238.8 1.8 convolution_bitcast_fusion.5
  240.8 1.8 convolution_bitcast_fusion.4
  243.3 1.8 convolution_bitcast_fusion.3
  245.4 1.7 convolution_bitcast_fusion.2
  247.3 1.8 convolution_bitcast_fusion.1
  249.4 1.7 convolution_bitcast_fusion
  251.2 2.1 multiply_add_fusion.35
  253.3 5.9 %multiply_add_fusion.34 = (f32[1,1044,128]{2,1,0:T(8,128)S(1)}, f32[1,1044,128]{2,1,0:T(8,128)S(1)}, f32[1,1044,128]{2,1,0:T(8,128)S(1)}, f32[1,1044,128]{2,1,0:T(8,128)S(1)}) fusion(f32[1044,12,128]{2,0,1:T(8,128)S(1)} %fusion.26, f32[]{:T(128)} %bitcast.28, f32[]{:T(128)} %bitcast.27, f32[]{:T(128)} %bitcast.26, f32[]{:T(128)} %bitcast.25, f32[]{:T(128)} %bitcast.24, ...), kind=kLoop, calls=%fused_computation.451 | loop fusion | flops 1870848 | bytes 5345316 | tf_op jit(solution)/shard_map/add | solution.py:116
  259.4 1.8 convolution_bitcast_fusion.23
  261.3 2.3 multiply_add_fusion.33
  263.6 5.9 %multiply_add_fusion.32 = (f32[1,1044,128]{2,1,0:T(8,128)S(1)}, f32[1,1044,128]{2,1,0:T(8,128)S(1)}, f32[1,1044,128]{2,1,0:T(8,128)S(1)}) fusion(f32[1044,12,128]{2,0,1:T(8,128)S(1)} %fusion.26, f32[]{:T(128)} %bitcast.54, f32[]{:T(128)} %bitcast.53, f32[]{:T(128)} %bitcast.52, f32[]{:T(128)} %bitcast.51, f32[]{:T(128)} %bitcast.76, f32[]{:T(128)} %bitcast.75, ...), kind=kLoop, calls=%fused_computation.449 | loop fusion | flops 2004480 | bytes 4810788 | tf_op jit(solution)/shard_map/add | solution.py:116
  269.7 1.7 convolution_bitcast_fusion.22
  271.5 2.0 multiply_add_fusion.31
  273.7 1.8 convolution_bitcast_fusion.21
  275.6 2.8 multiply_add_fusion.29
  278.6 2.0 convolution_bitcast_fusion.20
  281.1 1.8 convolution_bitcast_fusion.19
  283.1 1.8 convolution_bitcast_fusion.18
  285.2 1.8 convolution_bitcast_fusion.17
  287.3 1.8 convolution_bitcast_fusion.16
  289.3 1.8 convolution_bitcast_fusion.15
  292.2 1.7 convolution_bitcast_fusion.14
  295.2 1.8 convolution_bitcast_fusion.13
  298.2 1.7 convolution_bitcast_fusion.12
  301.2 3.2 fusion.32
  304.4 2.2 broadcast_in_dim.46
  307.7 2.7 fusion.29
  310.4 2.3 fusion.24
  312.8 170.6 %reduce-scatter.2.cloned.1.call-done = f32[128,2,128]{2,0,1:T(8,128)} async-done(((f32[4096,2,128]{2,0,1:T(8,128)}), f32[128,2,128]{2,0,1:T(8,128)}) %reduce-scatter.2.cloned.1.call-update) | async-done | bytes 131088 | tf_op jit(solution)/shard_map/reduce_scatter | solution.py:176
  483.4 1.7 copy.60
  (332 shorter events, 105.8 us)
Async XLA Ops:
  6.5 120.4 %copy-start.1 = (s32[1,1,2]{2,1,0:T(1,128)S(1)}, s32[1,1,2]{2,1,0:T(1,128)}, u32[]{:S(2)}) copy-start(s32[1,1,2]{2,1,0:T(1,128)} %param.7) | copy-start | bytes 28
  6.5 129.2 %copy-start = (f32[1,1,2,1024,2,128]{5,4,3,2,1,0:T(2,128)S(1)}, f32[1,1,2,1024,2,128]{5,4,3,2,1,0:T(2,128)}, u32[]{:S(2)}) copy-start(f32[1,1,2,1024,2,128]{5,4,3,2,1,0:T(2,128)} %param.4) | copy-start | bytes 6291460
  6.5 162.8 %all-gather.3.cloned.1.call-start = ((), (), s32[]{:S(2)}) async-start(), calls=%async_computation.2 | async-start | bytes 4325376 | tf_op jit(solution)/shard_map/all_gather | solution.py:156
  8.3 475.1 %reduce-scatter.2.cloned.1.call-start = ((), (), s32[]{:S(2)}) async-start(), calls=%async_computation.1 | async-start | bytes 4325376 | tf_op jit(solution)/shard_map/reduce_scatter | solution.py:176
  170.1 5.1 %collective-permute-start = (f32[10,2,128]{2,0,1:T(8,128)S(1)}, f32[10,2,128]{2,0,1:T(8,128)S(1)}, u32[]{:S(2)}, u32[]{:S(2)}) collective-permute-start(f32[10,2,128]{2,0,1:T(8,128)S(1)} %get-tuple-element.67), channel_id=1, source_target_pairs={{0,32},{32,64},{64,96},{1,33},{33,65},{65,97},{2,34},{34,66},{66,9... | collective-permute-start | bytes 30728 | tf_op jit(solution)/shard_map/ppermute | solution.py:23
  171.4 7.8 %collective-permute-start.1 = (f32[10,2,128]{2,0,1:T(8,128)S(1)}, f32[10,2,128]{2,0,1:T(8,128)S(1)}, u32[]{:S(2)}, u32[]{:S(2)}) collective-permute-start(f32[10,2,128]{2,0,1:T(8,128)S(1)} %get-tuple-element.66), channel_id=1, source_target_pairs={{32,0},{64,32},{96,64},{33,1},{65,33},{97,65},{34,2},{66,34},{98,6... | collective-permute-start | bytes 30728 | tf_op jit(solution)/shard_map/ppermute | solution.py:25
Sparse Core Ops, SparseCore 0:
  9.0 160.3 all-gather.2
  312.9 170.4 reduce-scatter.1
where the time goes:
time: 499 us; the launch traced here: 492 us
  waiting for transfers between devices  208 us (42%)
  other arithmetic  159 us (32%)
  matrix products  55.8 us (11%)
  local copies, waits for them, and re-layouts  34.5 us (7%)
  between operations  32.5 us (7%)
    reduce_scatter x1, waiting for transfers between devices, per_device(): lax.psum_scatter(dense_sums, 'dev', scatter_dimension=0, tiled=True)  171 us
    add x62, other arithmetic, strip_terms(): spatial_terms[number, 0] + spatial_terms[number, 1] * column_coords[None, :]  78 us
    dot_general x24, matrix products, strip_terms(): jnp.einsum('oi,tbic->tboc', matrix_rows, pieces, precision=lax.Precision....  43.2 us
    all_gather x1, waiting for transfers between devices, per_device(): region_band = lax.all_gather(coadd[0], 'dev', axis=0, tiled=True)  33.3 us
    add x4, other arithmetic, strip_terms(): sloped = sloped + spatial_terms[number, 2] * across_all[:, across, :]  23.3 us
    add x8, other arithmetic, strip_terms(): flat_part + (spatial_terms[number, 0] + spatial_terms[number, 1] * column...  18.4 us
    concatenate x1, local copies, waits for them, and re-layouts, per_device(): jnp.concatenate([extended[:half_width], region_band, extended[-half_width...  13.4 us
    dot_general x2, matrix products, strip_terms(): jnp.dot(flux_plane, wide_matrix, precision=lax.Precision.HIGHEST)  12.7 us
  transfers between devices with their start and end apart: 4, of which 3 were waited for; matrix products, arithmetic and copies ran while one was open for 23% of the time, Pallas kernels for 0%

commit v1 on v0

--- a/solution.py
+++ b/solution.py
@@ -153,7 +153,9 @@
         ]
     )
     wide_matrix = across_matrix(norm_values)
-    region_band = lax.all_gather(coadd[0], "dev", axis=0, tiled=True)
+    region_band = jnp.concatenate(
+        lax.all_to_all(jnp.stack([coadd[0]] * lax.axis_size("dev")), "dev", 0, 0), axis=0
+    )
     edge_rows = jnp.concatenate([region_band[:half_width], region_band[-half_width:]], axis=0)
     extended = padded_2(edge_rows, (("region", 0),), half_width)
     padded = jnp.concatenate([extended[:half_width], region_band, extended[-half_width:]], axis=0)

time: 499 us -> 481 us (0.964)
  waiting for transfers between devices: 208 us -> 176 us
  starting transfers between devices: 2.61 us -> 11.8 us
    all_gather x1 -> x0, waiting for transfers between devices: 33.3 us -> none  [per_device(): region_band = lax.all_gather(coadd[0], 'dev', axis=0, tiled=True)]
    all_to_all x0 -> x1, starting transfers between devices: none -> 9.02 us  [per_device(): lax.all_to_all(jnp.stack([coadd[0]] * lax.axis_size('dev')), 'dev', 0, 0)]
  transfers between devices with their start and end apart: 4 -> 4, of which waited for: 3 -> 2; matrix products, arithmetic and copies ran while one was open for 23% -> 24% of each run, Pallas kernels for 0% -> 0%
where the time goes in v1:
time: 481 us; the launch traced here: 473 us
  waiting for transfers between devices  176 us (37%)
  other arithmetic  158 us (33%)
  matrix products  55.8 us (12%)
  local copies, waits for them, and re-layouts  39.1 us (8%)
  between operations  32.8 us (7%)
  starting transfers between devices  11.8 us (2%)
    reduce_scatter x1, waiting for transfers between devices, per_device(): lax.psum_scatter(dense_sums, 'dev', scatter_dimension=0, tiled=True)  173 us
    add x62, other arithmetic, strip_terms(): spatial_terms[number, 0] + spatial_terms[number, 1] * column_coords[None, :]  77.3 us
    dot_general x24, matrix products, strip_terms(): jnp.einsum('oi,tbic->tboc', matrix_rows, pieces, precision=lax.Precision....  43.2 us
    add x4, other arithmetic, strip_terms(): sloped = sloped + spatial_terms[number, 2] * across_all[:, across, :]  23.6 us
    add x8, other arithmetic, strip_terms(): flat_part + (spatial_terms[number, 0] + spatial_terms[number, 1] * column...  18.2 us
    concatenate x1, local copies, waits for them, and re-layouts, per_device(): jnp.concatenate([extended[:half_width], region_band, extended[-half_width...  13.4 us
    dot_general x2, matrix products, strip_terms(): jnp.dot(flux_plane, wide_matrix, precision=lax.Precision.HIGHEST)  12.7 us
    unnamed x179, other arithmetic  10.2 us
  transfers between devices with their start and end apart: 4, of which 2 were waited for; matrix products, arithmetic and copies ran while one was open for 24% of the time, Pallas kernels for 0%

profile of v1, /device:TPU:0, one launch (start us, length us, event | category | flops | bytes accessed | tf_op | source)
XLA Modules:
  0.0 473.3 jit_solution(14494484929815873951)
XLA Ops:
  7.5 2.5 stack.885
  9.9 9.0 %all-to-all-start = ((f32[32,128,2,128]{3,1,2,0:T(8,128)}), f32[32,128,2,128]{3,1,2,0:T(8,128)}, u32[]{:S(2)}, u32[]{:S(2)}) async-start(f32[32,128,2,128]{3,1,2,0:T(8,128)} %stack.885), calls=%async_computation | async-start | bytes 8388608 | tf_op jit(solution)/shard_map/all_to_all | solution.py:157
  58.2 1.3 multiply_add_fusion.65
  59.5 1.3 multiply_add_fusion.66
  63.4 1.3 multiply_add_fusion.39
  65.9 1.3 multiply_add_fusion.60
  67.2 1.3 multiply_add_fusion.61
  87.2 1.3 multiply_add_fusion.46
  88.5 1.3 multiply_add_fusion.50
  105.9 1.3 multiply_add_fusion.92
  107.2 1.3 multiply_add_fusion.93
  113.3 1.4 multiply_add_fusion.75
  118.5 1.3 multiply_add_fusion.79
  124.2 1.3 multiply_add_fusion.88
  126.7 1.3 multiply_add_fusion.77
  145.7 2.5 copy.63
  148.2 2.0 copy-done
  150.1 1.4 collective-permute-start
  155.3 3.0 collective-permute-done.1
  158.3 13.4 %concatenate.6 = f32[4116,2,128]{2,0,1:T(8,128)} concatenate(f32[10,2,128]{2,0,1:T(8,128)S(1)} %collective-permute-done, f32[4096,2,128]{2,0,1:T(8,128)} %bitcast.1686, f32[10,2,128]{2,0,1:T(8,128)S(1)} %collective-permute-done.1), dimensions={0} | concatenate | bytes 8429568 | tf_op jit(solution)/shard_map/concatenate | solution.py:161
  171.7 6.2 %fusion.25 = f32[1044,12,128]{2,0,1:T(8,128)S(1)} fusion(f32[12,128,128]{2,1,0:T(8,128)S(1)} %bitcast.1687, f32[4116,2,128]{2,0,1:T(8,128)} %concatenate.6, s32[]{:T(128)S(6)} %select_n.126), kind=kOutput, calls=%fused_computation.402 | convolution fusion | flops 2463105024 | bytes 7737348 | tf_op jit(solution)/shard_map/dot_general | solution.py:99
  177.9 6.4 %fusion.26 = f32[1044,12,128]{2,0,1:T(8,128)S(1)} fusion(f32[12,128,128]{2,1,0:T(8,128)S(1)} %bitcast.1688, f32[4116,2,128]{2,0,1:T(8,128)} %concatenate.6, s32[]{:T(128)S(6)} %select_n.99), kind=kOutput, calls=%fused_computation.416 | convolution fusion | flops 2463105024 | bytes 7737348 | tf_op jit(solution)/shard_map/dot_general | solution.py:99
  184.4 2.1 multiply_add_fusion.17
  186.5 5.9 %multiply_add_fusion.16 = (f32[1,1044,128]{2,1,0:T(8,128)S(1)}, f32[1,1044,128]{2,1,0:T(8,128)S(1)}, f32[1,1044,128]{2,1,0:T(8,128)S(1)}, f32[1,1044,128]{2,1,0:T(8,128)S(1)}) fusion(f32[1044,12,128]{2,0,1:T(8,128)S(1)} %fusion.25, f32[]{:T(128)} %bitcast.316, f32[]{:T(128)} %bitcast.315, f32[]{:T(128)} %bitcast.314, f32[]{:T(128)} %bitcast.313, ...), kind=kLoop, calls=%fused_computation.433 | loop fusion | flops 1870848 | bytes 5345316 | tf_op jit(solution)/shard_map/add | solution.py:116
  192.5 2.1 convolution_bitcast_fusion.11
  194.7 2.2 multiply_add_fusion.15
  196.8 5.6 %multiply_add_fusion.14 = (f32[1,1044,128]{2,1,0:T(8,128)S(1)}, f32[1,1044,128]{2,1,0:T(8,128)S(1)}, f32[1,1044,128]{2,1,0:T(8,128)S(1)}) fusion(f32[1044,12,128]{2,0,1:T(8,128)S(1)} %fusion.25, f32[]{:T(128)} %bitcast.340, f32[]{:T(128)} %bitcast.339, f32[]{:T(128)} %bitcast.338, f32[]{:T(128)} %bitcast.337, f32[]{:T(128)} %bitcast.361, f32[]{:T(128)} %bitcast.360, ...), kind=kLoop, calls=%fused_computation.431 | loop fusion | flops 2004480 | bytes 4810788 | tf_op jit(solution)/shard_map/add | solution.py:116
  202.6 1.7 convolution_bitcast_fusion.10
  204.4 2.1 multiply_add_fusion.13
  206.7 1.8 convolution_bitcast_fusion.9
  208.5 2.8 multiply_add_fusion.11
  211.5 1.8 convolution_bitcast_fusion.8
  213.8 1.8 convolution_bitcast_fusion.7
  215.8 1.8 convolution_bitcast_fusion.6
  217.9 1.8 convolution_bitcast_fusion.5
  220.0 1.8 convolution_bitcast_fusion.4
  222.4 1.8 convolution_bitcast_fusion.3
  224.5 1.7 convolution_bitcast_fusion.2
  226.4 1.8 convolution_bitcast_fusion.1
  228.5 1.7 convolution_bitcast_fusion
  230.3 2.1 multiply_add_fusion.35
  232.4 6.1 %multiply_add_fusion.34 = (f32[1,1044,128]{2,1,0:T(8,128)S(1)}, f32[1,1044,128]{2,1,0:T(8,128)S(1)}, f32[1,1044,128]{2,1,0:T(8,128)S(1)}, f32[1,1044,128]{2,1,0:T(8,128)S(1)}) fusion(f32[1044,12,128]{2,0,1:T(8,128)S(1)} %fusion.26, f32[]{:T(128)} %bitcast.27, f32[]{:T(128)} %bitcast.26, f32[]{:T(128)} %bitcast.25, f32[]{:T(128)} %bitcast.24, f32[]{:T(128)} %bitcast.23, ...), kind=kLoop, calls=%fused_computation.451 | loop fusion | flops 1870848 | bytes 5345316 | tf_op jit(solution)/shard_map/add | solution.py:116
  238.7 1.8 convolution_bitcast_fusion.23
  240.6 2.2 multiply_add_fusion.33
  242.8 6.0 %multiply_add_fusion.32 = (f32[1,1044,128]{2,1,0:T(8,128)S(1)}, f32[1,1044,128]{2,1,0:T(8,128)S(1)}, f32[1,1044,128]{2,1,0:T(8,128)S(1)}) fusion(f32[1044,12,128]{2,0,1:T(8,128)S(1)} %fusion.26, f32[]{:T(128)} %bitcast.53, f32[]{:T(128)} %bitcast.52, f32[]{:T(128)} %bitcast.51, f32[]{:T(128)} %bitcast.50, f32[]{:T(128)} %bitcast.75, f32[]{:T(128)} %bitcast.74, ...), kind=kLoop, calls=%fused_computation.449 | loop fusion | flops 2004480 | bytes 4810788 | tf_op jit(solution)/shard_map/add | solution.py:116
  249.0 1.7 convolution_bitcast_fusion.22
  250.8 2.0 multiply_add_fusion.31
  253.0 1.8 convolution_bitcast_fusion.21
  254.9 2.8 multiply_add_fusion.29
  257.8 2.0 convolution_bitcast_fusion.20
  260.3 1.8 convolution_bitcast_fusion.19
  262.4 1.8 convolution_bitcast_fusion.18
  264.4 1.8 convolution_bitcast_fusion.17
  266.5 1.8 convolution_bitcast_fusion.16
  268.5 1.8 convolution_bitcast_fusion.15
  271.4 1.7 convolution_bitcast_fusion.14
  274.4 1.8 convolution_bitcast_fusion.13
  277.4 1.7 convolution_bitcast_fusion.12
  280.4 3.2 fusion.32
  283.6 2.2 broadcast_in_dim.46
  286.9 2.7 fusion.29
  289.6 2.3 fusion.24
  292.0 172.6 %reduce-scatter.2.cloned.1.call-done = f32[128,2,128]{2,0,1:T(8,128)} async-done(((f32[4096,2,128]{2,0,1:T(8,128)}), f32[128,2,128]{2,0,1:T(8,128)}) %reduce-scatter.2.cloned.1.call-update) | async-done | bytes 131088 | tf_op jit(solution)/shard_map/reduce_scatter | solution.py:178
  464.6 1.7 copy.89
  (337 shorter events, 107.2 us)
Async XLA Ops:
  9.9 16.9 %copy-start.2 = (f32[1,1,2,31,3]{3,2,4,1,0:T(2,128)S(1)}, f32[1,1,2,31,3]{3,2,4,1,0:T(2,128)}, u32[]{:S(2)}) copy-start(f32[1,1,2,31,3]{3,2,4,1,0:T(2,128)} %param.6) | copy-start | bytes 2236
  9.9 126.7 %copy-start.3 = (s32[1,1,2]{2,1,0:T(1,128)S(1)}, s32[1,1,2]{2,1,0:T(1,128)}, u32[]{:S(2)}) copy-start(s32[1,1,2]{2,1,0:T(1,128)} %param.7) | copy-start | bytes 28
  9.9 135.5 %copy-start.1 = (f32[1,1,2,1024,2,128]{5,4,3,2,1,0:T(2,128)S(1)}, f32[1,1,2,1024,2,128]{5,4,3,2,1,0:T(2,128)}, u32[]{:S(2)}) copy-start(f32[1,1,2,1024,2,128]{5,4,3,2,1,0:T(2,128)} %param.4) | copy-start | bytes 6291460
  9.9 135.8 %all-to-all-start = ((f32[32,128,2,128]{3,1,2,0:T(8,128)}), f32[32,128,2,128]{3,1,2,0:T(8,128)}, u32[]{:S(2)}, u32[]{:S(2)}) async-start(f32[32,128,2,128]{3,1,2,0:T(8,128)} %stack.885), calls=%async_computation | async-start | bytes 8388608 | tf_op jit(solution)/shard_map/all_to_all | solution.py:157
  19.0 445.6 %reduce-scatter.2.cloned.1.call-start = ((), (), s32[]{:S(2)}) async-start(), calls=%async_computation.2 | async-start | bytes 4325376 | tf_op jit(solution)/shard_map/reduce_scatter | solution.py:178
  148.2 2.0 copy-start
  150.1 5.2 %collective-permute-start = (f32[10,2,128]{2,0,1:T(8,128)S(1)}, f32[10,2,128]{2,0,1:T(8,128)S(1)}, u32[]{:S(2)}, u32[]{:S(2)}) collective-permute-start(f32[10,2,128]{2,0,1:T(8,128)S(1)} %get-tuple-element.67), channel_id=1, source_target_pairs={{0,32},{32,64},{64,96},{1,33},{33,65},{65,97},{2,34},{34,66},{66,9... | collective-permute-start | bytes 30728 | tf_op jit(solution)/shard_map/ppermute | solution.py:23
  151.6 6.7 %collective-permute-start.1 = (f32[10,2,128]{2,0,1:T(8,128)S(1)}, f32[10,2,128]{2,0,1:T(8,128)S(1)}, u32[]{:S(2)}, u32[]{:S(2)}) collective-permute-start(f32[10,2,128]{2,0,1:T(8,128)S(1)} %get-tuple-element.66), channel_id=1, source_target_pairs={{32,0},{64,32},{96,64},{33,1},{65,33},{97,65},{34,2},{66,34},{98,6... | collective-permute-start | bytes 30728 | tf_op jit(solution)/shard_map/ppermute | solution.py:25
Sparse Core Ops, SparseCore 0:
  292.1 172.4 reduce-scatter.1
